TPU v7x, 1024 devices: a whole 8x8x8 slice. The times are simulated.
1024 devices in a mesh: space: 32 (over y, z_lo, core), band: 32 (over z_hi, x).
Axes of the slice: x: 8, y: 8, z: 8 (z_hi: 4, z_lo: 2; z = z_hi * 2 + z_lo), core: 2. Of those that a mesh axis runs over, the one named last changes fastest.
Arguments:
- orbitals: float32 [512, 64, 24, 128], P('band', 'space'), may hold values from -6 to 6
- potential: float32 [64, 24, 128], P('space'), may hold values from 0 to 2
- rotation: float32 [512, 512], P(None, 'band'), may hold values from -0.25 to 0.25
Outputs:
- gram: float32 [512, 512], P('band', 'space')
- projected: float32 [512, 512], P('band', 'space')
- rotated: float32 [512, 64, 24, 128], P('band', 'space')
All inputs are finite; a program needn't handle non-finite values.
Results may differ from a plain program's by a relative error of at most 0.004.
Values may be sent and summed in bfloat16 or wider, within the bound.
A program may use at most 32 MiB of HBM per device.

v0:
```python
import jax
import jax.numpy as jnp
from jax import lax
from jax.sharding import PartitionSpec as P

ORB = 512
DEGREE = 8


FILTER_LOW = 2.0
FILTER_HIGH = 8.0
LOWER_EDGE = 0.0


def extended(value, sides, width):
    for axis, dim in sides:
        size, length = (lax.axis_size(axis), value.shape[dim])
        up = [(i, (i + 1) % size) for i in range(size - 1)]
        down = [(j, i) for i, j in up]
        last = lax.slice_in_dim(value, length - width, length, axis=dim)
        leading = lax.slice_in_dim(value, 0, width, axis=dim)
        before = lax.ppermute(last, axis, up)
        after = lax.ppermute(leading, axis, down)
        value = jnp.concatenate([before, value, after], axis=dim)
    return value


def hamilton(values, potential):
    padded = extended(values, (("space", 1),), 1)
    side_pad = jnp.pad(values, ((0, 0), (0, 0), (1, 1), (1, 1)))
    neighbours = padded[:, 2:] + padded[:, :-2]
    neighbours = neighbours + side_pad[:, :, 2:, 1:-1] + side_pad[:, :, :-2, 1:-1]
    neighbours = neighbours + side_pad[:, :, 1:-1, 2:] + side_pad[:, :, 1:-1, :-2]
    return -0.5 * (neighbours - 6.0 * values) + potential[None] * values


def chebyshev(start_values, potential):
    half_width = (FILTER_HIGH - FILTER_LOW) / 2.0
    centre = (FILTER_HIGH + FILTER_LOW) / 2.0
    first = half_width / (LOWER_EDGE - centre)
    ratio_now = first
    previous = start_values
    current = first / half_width * (hamilton(start_values, potential) - centre * start_values)
    for degree_step in range(DEGREE - 1):
        ratio_next = 1.0 / (2.0 / first - ratio_now)
        upcoming = (
            2.0 * ratio_next / half_width * (hamilton(current, potential) - centre * current)
            - ratio_now * ratio_next * previous
        )
        previous = current
        current = upcoming
        ratio_now = ratio_next
    return current


def contract_nodes(left, right):
    return lax.dot_general(
        left, right, (((1,), (1,)), ((), ())), preferred_element_type=jnp.float32
    )


def shards(orbitals, potential, rotation):
    local_cols = orbitals.shape[0]
    filtered_b = chebyshev(orbitals, potential).astype(jnp.bfloat16)
    applied_b = hamilton(filtered_b.astype(jnp.float32), potential).astype(jnp.bfloat16)
    flat_f = filtered_b.reshape(local_cols, -1)
    flat_h = applied_b.reshape(local_cols, -1)
    rotation_b = rotation.astype(jnp.bfloat16)
    gathered = lax.all_gather(filtered_b, "band", axis=0, tiled=True)
    flat_all = gathered.reshape(ORB, -1)
    gram_part = contract_nodes(flat_all, flat_f)
    proj_part = contract_nodes(flat_all, flat_h)
    rotated = lax.dot_general(
        rotation_b, flat_all, (((0,), (0,)), ((), ())), preferred_element_type=jnp.float32
    )
    partials = jnp.stack([gram_part, proj_part], 1)
    owned_cols = ORB // lax.axis_size("space")
    summed = lax.psum(partials, "space")
    mine = lax.dynamic_slice_in_dim(summed, lax.axis_index("space") * owned_cols, owned_cols, 0)
    gram = mine[:, 0, :].T
    projected = mine[:, 1, :].T
    return (gram, projected, rotated.reshape(orbitals.shape))


def solution(mesh):
    placed = (P("band", "space", None, None), P("space", None, None), P(None, "band"))
    return jax.shard_map(
        shards,
        mesh=mesh,
        in_specs=placed,
        out_specs=(P("band", "space"), P("band", "space"), P("band", "space", None, None)),
        check_vma=False,
    )
```

profile of v0, /device:TPU:1, one launch (start us, length us, event | category | flops | bytes accessed | tf_op | source)
XLA Modules:
  0.0 467.5 jit_solution(16651306904039555324)
XLA Ops:
  8.4 6.3 %collective-permute-start.1 = (f32[16,1,24,128]{3,0,2,1:T(8,128)S(1)}, f32[16,1,24,128]{3,0,2,1:T(8,128)S(1)}, u32[]{:S(2)}, u32[]{:S(2)}) collective-permute-start(f32[16,1,24,128]{3,0,2,1:T(8,128)S(1)} %get-tuple-element.22), channel_id=1, source_target_pairs={{0,32},{32,64},{64,96},{96,128},{128,160},{160,192},{192,224},{224... | collective-permute-start | bytes 589832 | tf_op jit(solution)/shard_map/ppermute | solution.py:22
  14.7 11.1 %collective-permute-start = (f32[16,1,24,128]{3,0,2,1:T(8,128)S(1)}, f32[16,1,24,128]{3,0,2,1:T(8,128)S(1)}, u32[]{:S(2)}, u32[]{:S(2)}) collective-permute-start(f32[16,1,24,128]{3,0,2,1:T(8,128)S(1)} %get-tuple-element.21), channel_id=1, source_target_pairs={{32,0},{64,32},{96,64},{128,96},{160,128},{192,160},{224,192},{256... | collective-permute-start | bytes 589832 | tf_op jit(solution)/shard_map/ppermute | solution.py:23
  29.8 2.4 collective-permute-start.2
  33.3 3.5 collective-permute-done.2
  40.2 2.4 collective-permute-start.4
  44.6 2.5 collective-permute-done.4
  49.5 2.4 collective-permute-start.6
  51.9 2.3 collective-permute-done.7
  54.2 2.3 collective-permute-done.6
  59.0 2.2 collective-permute-start.8
  61.2 2.5 collective-permute-done.9
  63.7 2.3 collective-permute-done.8
  68.5 2.2 collective-permute-start.10
  71.1 4.4 collective-permute-done.10
  77.8 2.4 collective-permute-start.12
  80.4 4.4 collective-permute-done.12
  87.1 2.4 collective-permute-start.14
  89.7 4.4 collective-permute-done.14
  98.1 2.4 collective-permute-start.16
  100.5 147.9 %all-gather.2.cloned.1.call-done = bf16[512,2,24,128]{3,0,2,1:T(8,128)(2,1)} async-done(((bf16[16,2,24,128]{3,0,2,1:T(8,128)(2,1)}), bf16[512,2,24,128]{3,0,2,1:T(8,128)(2,1)}) %all-gather.2.cloned.1.call-update) | async-done | bytes 6291472 | tf_op jit(solution)/shard_map/all_gather | solution.py:69
  248.4 4.7 convolution_bitcast_fusion.2
  255.5 8.7 %copy.24 = bf16[512,2,24,128]{0,3,2,1:T(8,128)(2,1)} copy(bf16[512,2,24,128]{3,0,2,1:T(8,128)(2,1)} %all-gather.2.cloned.1.call-done) | data formatting | bytes 12582912 | tf_op jit(solution)/shard_map/all_gather | solution.py:69
  264.1 4.5 convolution_bitcast_fusion
  269.5 189.8 %all-reduce.11.cloned.1.call-done = f32[512,2,16]{0,2,1:T(8,128)} async-done(((f32[512,2,16]{0,2,1:T(8,128)}), f32[512,2,16]{0,2,1:T(8,128)}) %all-reduce.11.cloned.1.call-update) | async-done | bytes 65552 | tf_op jit(solution)/shard_map/psum | solution.py:78
  (50 shorter events, 32.8 us)
Async XLA Ops:
  7.2 40.0 %copy-start.1 = (f32[2,24,128]{2,1,0:T(8,128)S(1)}, f32[2,24,128]{2,1,0:T(8,128)}, u32[]{:S(2)}) copy-start(f32[2,24,128]{2,1,0:T(8,128)} %param.4) | copy-start | bytes 73732
  7.2 241.2 %all-gather.2.cloned.1.call-start = ((), (), s32[]{:S(2)}) async-start(), calls=%async_computation | async-start | bytes 6488064 | tf_op jit(solution)/shard_map/all_gather | solution.py:69
  8.4 17.4 %collective-permute-start.1 = (f32[16,1,24,128]{3,0,2,1:T(8,128)S(1)}, f32[16,1,24,128]{3,0,2,1:T(8,128)S(1)}, u32[]{:S(2)}, u32[]{:S(2)}) collective-permute-start(f32[16,1,24,128]{3,0,2,1:T(8,128)S(1)} %get-tuple-element.22), channel_id=1, source_target_pairs={{0,32},{32,64},{64,96},{96,128},{128,160},{160,192},{192,224},{224... | collective-permute-start | bytes 589832 | tf_op jit(solution)/shard_map/ppermute | solution.py:22
  14.7 12.1 %collective-permute-start = (f32[16,1,24,128]{3,0,2,1:T(8,128)S(1)}, f32[16,1,24,128]{3,0,2,1:T(8,128)S(1)}, u32[]{:S(2)}, u32[]{:S(2)}) collective-permute-start(f32[16,1,24,128]{3,0,2,1:T(8,128)S(1)} %get-tuple-element.21), channel_id=1, source_target_pairs={{32,0},{64,32},{96,64},{128,96},{160,128},{192,160},{224,192},{256... | collective-permute-start | bytes 589832 | tf_op jit(solution)/shard_map/ppermute | solution.py:23
  27.9 5.4 %collective-permute-start.3 = (f32[16,1,24,128]{3,0,2,1:T(8,128)S(1)}, f32[16,1,24,128]{3,0,2,1:T(8,128)S(1)}, u32[]{:S(2)}, u32[]{:S(2)}) collective-permute-start(f32[16,1,24,128]{3,0,2,1:T(8,128)S(1)} %get-tuple-element.20), channel_id=1, source_target_pairs={{0,32},{32,64},{64,96},{96,128},{128,160},{160,192},{192,224},{224... | collective-permute-start | bytes 589832 | tf_op jit(solution)/shard_map/ppermute | solution.py:22
  29.8 7.0 %collective-permute-start.2 = (f32[16,1,24,128]{3,0,2,1:T(8,128)S(1)}, f32[16,1,24,128]{3,0,2,1:T(8,128)S(1)}, u32[]{:S(2)}, u32[]{:S(2)}) collective-permute-start(f32[16,1,24,128]{3,0,2,1:T(8,128)S(1)} %get-tuple-element.19), channel_id=1, source_target_pairs={{32,0},{64,32},{96,64},{128,96},{160,128},{192,160},{224,192},{256... | collective-permute-start | bytes 589832 | tf_op jit(solution)/shard_map/ppermute | solution.py:23
  38.3 6.4 %collective-permute-start.5 = (f32[16,1,24,128]{3,0,2,1:T(8,128)S(1)}, f32[16,1,24,128]{3,0,2,1:T(8,128)S(1)}, u32[]{:S(2)}, u32[]{:S(2)}) collective-permute-start(f32[16,1,24,128]{3,0,2,1:T(8,128)S(1)} %get-tuple-element.18), channel_id=1, source_target_pairs={{0,32},{32,64},{64,96},{96,128},{128,160},{160,192},{192,224},{224... | collective-permute-start | bytes 589832 | tf_op jit(solution)/shard_map/ppermute | solution.py:22
  40.2 7.0 %collective-permute-start.4 = (f32[16,1,24,128]{3,0,2,1:T(8,128)S(1)}, f32[16,1,24,128]{3,0,2,1:T(8,128)S(1)}, u32[]{:S(2)}, u32[]{:S(2)}) collective-permute-start(f32[16,1,24,128]{3,0,2,1:T(8,128)S(1)} %get-tuple-element.17), channel_id=1, source_target_pairs={{32,0},{64,32},{96,64},{128,96},{160,128},{192,160},{224,192},{256... | collective-permute-start | bytes 589832 | tf_op jit(solution)/shard_map/ppermute | solution.py:23
  47.6 6.6 %collective-permute-start.7 = (f32[16,1,24,128]{3,0,2,1:T(8,128)S(1)}, f32[16,1,24,128]{3,0,2,1:T(8,128)S(1)}, u32[]{:S(2)}, u32[]{:S(2)}) collective-permute-start(f32[16,1,24,128]{3,0,2,1:T(8,128)S(1)} %get-tuple-element.16), channel_id=1, source_target_pairs={{0,32},{32,64},{64,96},{96,128},{128,160},{160,192},{192,224},{224... | collective-permute-start | bytes 589832 | tf_op jit(solution)/shard_map/ppermute | solution.py:22
  49.5 7.0 %collective-permute-start.6 = (f32[16,1,24,128]{3,0,2,1:T(8,128)S(1)}, f32[16,1,24,128]{3,0,2,1:T(8,128)S(1)}, u32[]{:S(2)}, u32[]{:S(2)}) collective-permute-start(f32[16,1,24,128]{3,0,2,1:T(8,128)S(1)} %get-tuple-element.15), channel_id=1, source_target_pairs={{32,0},{64,32},{96,64},{128,96},{160,128},{192,160},{224,192},{256... | collective-permute-start | bytes 589832 | tf_op jit(solution)/shard_map/ppermute | solution.py:23
  56.9 6.8 %collective-permute-start.9 = (f32[16,1,24,128]{3,0,2,1:T(8,128)S(1)}, f32[16,1,24,128]{3,0,2,1:T(8,128)S(1)}, u32[]{:S(2)}, u32[]{:S(2)}) collective-permute-start(f32[16,1,24,128]{3,0,2,1:T(8,128)S(1)} %get-tuple-element.14), channel_id=1, source_target_pairs={{0,32},{32,64},{64,96},{96,128},{128,160},{160,192},{192,224},{224... | collective-permute-start | bytes 589832 | tf_op jit(solution)/shard_map/ppermute | solution.py:22
  59.0 7.0 %collective-permute-start.8 = (f32[16,1,24,128]{3,0,2,1:T(8,128)S(1)}, f32[16,1,24,128]{3,0,2,1:T(8,128)S(1)}, u32[]{:S(2)}, u32[]{:S(2)}) collective-permute-start(f32[16,1,24,128]{3,0,2,1:T(8,128)S(1)} %get-tuple-element.13), channel_id=1, source_target_pairs={{32,0},{64,32},{96,64},{128,96},{160,128},{192,160},{224,192},{256... | collective-permute-start | bytes 589832 | tf_op jit(solution)/shard_map/ppermute | solution.py:23
  66.4 4.7 %collective-permute-start.11 = (f32[16,1,24,128]{3,0,2,1:T(8,128)S(1)}, f32[16,1,24,128]{3,0,2,1:T(8,128)S(1)}, u32[]{:S(2)}, u32[]{:S(2)}) collective-permute-start(f32[16,1,24,128]{3,0,2,1:T(8,128)S(1)} %get-tuple-element.12), channel_id=1, source_target_pairs={{0,32},{32,64},{64,96},{96,128},{128,160},{160,192},{192,224},{224... | collective-permute-start | bytes 589832 | tf_op jit(solution)/shard_map/ppermute | solution.py:22
  68.5 7.0 %collective-permute-start.10 = (f32[16,1,24,128]{3,0,2,1:T(8,128)S(1)}, f32[16,1,24,128]{3,0,2,1:T(8,128)S(1)}, u32[]{:S(2)}, u32[]{:S(2)}) collective-permute-start(f32[16,1,24,128]{3,0,2,1:T(8,128)S(1)} %get-tuple-element.11), channel_id=1, source_target_pairs={{32,0},{64,32},{96,64},{128,96},{160,128},{192,160},{224,192},{256... | collective-permute-start | bytes 589832 | tf_op jit(solution)/shard_map/ppermute | solution.py:23
  75.8 4.5 collective-permute-start.13
  77.8 7.0 %collective-permute-start.12 = (f32[16,1,24,128]{3,0,2,1:T(8,128)S(1)}, f32[16,1,24,128]{3,0,2,1:T(8,128)S(1)}, u32[]{:S(2)}, u32[]{:S(2)}) collective-permute-start(f32[16,1,24,128]{3,0,2,1:T(8,128)S(1)} %get-tuple-element.9), channel_id=1, source_target_pairs={{32,0},{64,32},{96,64},{128,96},{160,128},{192,160},{224,192},{256... | collective-permute-start | bytes 589832 | tf_op jit(solution)/shard_map/ppermute | solution.py:23
  85.1 4.5 collective-permute-start.15
  87.1 7.0 %collective-permute-start.14 = (f32[16,1,24,128]{3,0,2,1:T(8,128)S(1)}, f32[16,1,24,128]{3,0,2,1:T(8,128)S(1)}, u32[]{:S(2)}, u32[]{:S(2)}) collective-permute-start(f32[16,1,24,128]{3,0,2,1:T(8,128)S(1)} %get-tuple-element.7), channel_id=1, source_target_pairs={{32,0},{64,32},{96,64},{128,96},{160,128},{192,160},{224,192},{256... | collective-permute-start | bytes 589832 | tf_op jit(solution)/shard_map/ppermute | solution.py:23
  95.1 364.2 %all-reduce.11.cloned.1.call-start = ((), (), s32[]{:S(2)}) async-start(), calls=%async_computation.1 | async-start | bytes 131072 | tf_op jit(solution)/shard_map/psum | solution.py:78
  96.1 156.9 %collective-permute-start.17 = (f32[16,1,24,128]{3,0,2,1:T(8,128)S(1)}, f32[16,1,24,128]{3,0,2,1:T(8,128)S(1)}, u32[]{:S(2)}, u32[]{:S(2)}) collective-permute-start(f32[16,1,24,128]{3,0,2,1:T(8,128)S(1)} %get-tuple-element.24), channel_id=1, source_target_pairs={{0,32},{32,64},{64,96},{96,128},{128,160},{160,192},{192,224},{224... | collective-permute-start | bytes 589832 | tf_op jit(solution)/shard_map/ppermute | solution.py:22
  98.1 155.0 %collective-permute-start.16 = (f32[16,1,24,128]{3,0,2,1:T(8,128)S(1)}, f32[16,1,24,128]{3,0,2,1:T(8,128)S(1)}, u32[]{:S(2)}, u32[]{:S(2)}) collective-permute-start(f32[16,1,24,128]{3,0,2,1:T(8,128)S(1)} %get-tuple-element.23), channel_id=1, source_target_pairs={{32,0},{64,32},{96,64},{128,96},{160,128},{192,160},{224,192},{256... | collective-permute-start | bytes 589832 | tf_op jit(solution)/shard_map/ppermute | solution.py:23
  248.4 4.7 %copy-start = (bf16[512,2,24,128]{3,0,2,1:T(8,128)(2,1)S(1)}, bf16[512,2,24,128]{3,0,2,1:T(8,128)(2,1)}, u32[]{:S(2)}) copy-start(bf16[512,2,24,128]{3,0,2,1:T(8,128)(2,1)} %all-gather.2.cloned.1.call-done) | copy-start | bytes 18874372
  255.5 8.7 %copy-start.2 = (f32[512,16]{0,1:T(8,128)S(1)}, f32[512,16]{0,1:T(8,128)}, u32[]{:S(2)}) copy-start(f32[512,16]{0,1:T(8,128)} %param.5) | copy-start | bytes 98308
Sparse Core Ops, SparseCore 0:
  95.2 153.0 all-gather.1
  255.6 203.6 all-reduce.10
where the time goes:
time: 469 us; the launch traced here: 468 us
  waiting for transfers between devices  370 us (79%)
  starting transfers between devices  52.1 us (11%)
  between operations  14.4 us (3%)
  local copies, waits for them, and re-layouts  13.2 us (3%)
  matrix products  10.9 us (2%)
  other arithmetic  6.58 us (1%)
    psum x1, waiting for transfers between devices, shards(): summed = lax.psum(partials, 'space')  190 us
    all_gather x1, waiting for transfers between devices, shards(): gathered = lax.all_gather(filtered_b, 'band', axis=0, tiled=True)  148 us
    ppermute x9, starting transfers between devices, extended(): after = lax.ppermute(leading, axis, down)  30 us
    ppermute x9, waiting for transfers between devices, extended(): after = lax.ppermute(leading, axis, down)  24.9 us
    ppermute x9, starting transfers between devices, extended(): before = lax.ppermute(last, axis, up)  22 us
  transfers between devices with their start and end apart: 20, of which 17 were waited for; matrix products, arithmetic and copies ran while one was open for 4% of the time, Pallas kernels for 0%

commit v1 on v0

v1 whole, which is shorter than its diff:
```python
import functools

import jax
import jax.numpy as jnp
from jax import lax
from jax.experimental import pallas as pl
from jax.experimental.pallas import tpu as pltpu
from jax.sharding import PartitionSpec as P

DEGREE = 8
FILTER_LOW = 2.0
FILTER_HIGH = 8.0
LOWER_EDGE = 0.0
MESH = pl.DeviceIdType.MESH
VMEM = pltpu.VMEM
F32 = jnp.float32
BF16 = jnp.bfloat16

ZH = 4
Z = 8
NY = 24
NZ = 128
CHUNKS = 3
ROWS = NY // CHUNKS


def steps():
    half_width = (FILTER_HIGH - FILTER_LOW) / 2.0
    centre = (FILTER_HIGH + FILTER_LOW) / 2.0
    first = half_width / (LOWER_EDGE - centre)
    ratio = first
    out = [(first / half_width, 0.0)]
    for _ in range(DEGREE - 1):
        ratio_next = 1.0 / (2.0 / first - ratio)
        out.append((2.0 * ratio_next / half_width, ratio * ratio_next))
        ratio = ratio_next
    return centre, out


def position(n_x):
    bi, si = lax.axis_index("band"), lax.axis_index("space")
    zh, x = bi // n_x, lax.rem(bi, n_x)
    y, q = si // 4, lax.rem(si, 4)
    zl, c = q // 2, lax.rem(q, 2)
    return zh, x, y, q, zl, c


def send(src, dst, send_sem, recv_sem, band, space):
    copy = pltpu.make_async_remote_copy(
        src_ref=src,
        dst_ref=dst,
        send_sem=send_sem,
        recv_sem=recv_sem,
        device_id={"band": band, "space": space},
        device_id_type=MESH,
    )
    return copy


def side_sum(v):
    n = v.shape[0]
    row = lax.broadcasted_iota(jnp.int32, (1, NY, 1), 1)
    lane = lax.broadcasted_iota(jnp.int32, (1, NZ), 1)
    above = jnp.where(row == 0, 0.0, pltpu.roll(v, 1, 1))
    below = jnp.where(row == NY - 1, 0.0, pltpu.roll(v, NY - 1, 1))
    flat = v.reshape(n * NY, NZ)
    left = jnp.where(lane == 0, 0.0, pltpu.roll(flat, 1, 1))
    right = jnp.where(lane == NZ - 1, 0.0, pltpu.roll(flat, NZ - 1, 1))
    return (above + below) + (left + right).reshape(n, NY, NZ)


def filter_kernel(
    n_x, n_y, orb, pot, rt, f1, h1, rt_all,
    ext, work, pv, edge, fb, hb, fr, hr,
    a_send, a_recv, b_send, b_recv, v_send, v_recv, d_send, d_recv,
    f_send, f_recv, h_send, h_recv, r_send, r_recv,
):
    zh, x, y, q, zl, c = position(n_x)
    z = zh * 2 + zl
    me_b, me_s = zh * n_x + x, y * 4 + q
    low, high = y > 0, y < n_y - 1

    @pl.when(y == 0)
    def _():
        for o in range(4):
            ext[o, 0:8] = jnp.zeros((8, NY, NZ), F32)
        pv[0] = jnp.zeros((2, 2, 2, NY, NZ), F32)
        edge[0] = jnp.zeros((4, NY, NZ), F32)

    @pl.when(y == n_y - 1)
    def _():
        for o in range(4):
            ext[o, 16:24] = jnp.zeros((8, NY, NZ), F32)
        pv[2] = jnp.zeros((2, 2, 2, NY, NZ), F32)
        edge[1] = jnp.zeros((4, NY, NZ), F32)

    def along_z(d):
        other = lax.rem(z + d, Z)
        return other, (other // 2) * n_x + x, y * 4 + lax.rem(other, 2) * 2 + c

    barrier = pltpu.get_barrier_semaphore()

    def greet(band, space):
        pl.semaphore_signal(
            barrier, inc=1, device_id={"band": band, "space": space}, device_id_type=MESH
        )

    for d in range(1, Z):
        _, band, space = along_z(d)
        greet(band, space)
    greet(me_b, y * 4 + zl * 2 + (1 - c))
    greet(me_b, y * 4 + (1 - zl) * 2 + (1 - c))

    @pl.when(low)
    def _():
        greet(me_b, me_s - 4)

    @pl.when(high)
    def _():
        greet(me_b, me_s + 4)

    pl.semaphore_wait(barrier, Z + 1 + low.astype(jnp.int32) + high.astype(jnp.int32))

    mate = y * 4 + (1 - zl) * 2 + c
    core = y * 4 + zl * 2 + (1 - c)
    v_mate = send(pot, pv.at[1, zl, c], v_send.at[0], v_recv.at[0], me_b, mate)
    v_mate.start()

    def a_copy(o, d):
        to = lax.rem(q + d, 4)
        return send(
            orb.at[4 * to + o], ext.at[o, pl.ds(8 + 2 * q, 2)],
            a_send.at[o, d - 1], a_recv.at[o, d - 1], me_b, y * 4 + to,
        )

    for o in range(4):
        for d in (2, 1, 3):
            a_copy(o, d).start()

    def r_copy(d):
        to = lax.rem(zh + d, ZH)
        return send(
            rt, rt_all.at[pl.ds(pl.multiple_of(16 * zh, 16), 16)],
            r_send.at[d - 1], r_recv.at[d - 1], to * n_x + x, me_s,
        )

    pv[1, zl, c] = pot[...]
    for o in range(4):
        ext[o, pl.ds(8 + 2 * q, 2)] = orb[4 * q + o]
    rt_all[pl.ds(pl.multiple_of(16 * zh, 16), 16)] = rt[...]

    v_mate.wait_recv()
    v_up = send(pv.at[1, :, c], pv.at[0, :, c], v_send.at[1], v_recv.at[1], me_b, me_s + 4)
    v_down = send(pv.at[1, :, c], pv.at[2, :, c], v_send.at[2], v_recv.at[2], me_b, me_s - 4)

    @pl.when(high)
    def _():
        v_up.start()

    @pl.when(low)
    def _():
        v_down.start()

    def up(o):
        return send(
            ext.at[o, 8:16], ext.at[o, 0:8], b_send.at[o, 0], b_recv.at[o, 0], me_b, me_s + 4
        )

    def down(o):
        return send(
            ext.at[o, 8:16], ext.at[o, 16:24], b_send.at[o, 1], b_recv.at[o, 1], me_b, me_s - 4
        )

    for o in range(4):
        for d in (2, 1, 3):
            a_copy(o, d).wait_recv()

        @pl.when(high)
        def _():
            up(o).start()

        @pl.when(low)
        def _():
            down(o).start()

    for d in range(1, ZH):
        r_copy(d).start()

    @pl.when(low)
    def _():
        v_up.wait_recv()

    @pl.when(high)
    def _():
        v_down.wait_recv()

    v_core = send(pv.at[:, :, c], pv.at[:, :, c], v_send.at[3], v_recv.at[3], me_b, core)
    v_core.start()
    send(
        pv.at[:, :, 1 - c], pv.at[:, :, 1 - c], v_send.at[3], v_recv.at[3], me_b, core
    ).wait_recv()

    centre, coefficients = steps()
    flag_low = jnp.where(low, 1.0, 0.0).astype(F32)
    flag_high = jnp.where(high, 1.0, 0.0).astype(F32)

    def potential(p):
        return pv[p // 8, lax.rem(p, 8) // 4, lax.rem(p, 4) // 2, lax.rem(p, 2)]

    def apply(src, s0, dst, d0, first_plane, count, scale, back, shift, clip):
        def body(i, carry):
            p = first_plane + 2 * i
            v = src[pl.ds(s0, 2), pl.ds(p - 1, 4)]
            if back != 0.0:
                old = dst[pl.ds(d0, 2), pl.ds(p, 2)]
            for k in range(2):
                now = v[:, k + 1]
                near = side_sum(now) + (v[:, k] + v[:, k + 2])
                level = (potential(p + k) + shift) * scale
                new = near * (-0.5 * scale) + level[None] * now
                if back != 0.0:
                    new = new - back * old[:, k]
                if clip:
                    here = p + k
                    flag = jnp.where(here < 8, flag_low, jnp.where(here >= 16, flag_high, 1.0))
                    new = new * flag
                dst[pl.ds(d0, 2), p + k] = new
            return carry

        lax.fori_loop(0, count // 2, body, 0)

    def f_copy(pair, d):
        other, band, space = along_z(d)
        return send(
            fb.at[pair, other], fr.at[z, pair],
            f_send.at[pair, d - 1], f_recv.at[pair, d - 1], band, space,
        )

    def h_copy(pair, d):
        other, band, space = along_z(d)
        return send(
            hb.at[pair, other], hr.at[z, pair],
            h_send.at[pair, d - 1], h_recv.at[pair, d - 1], band, space,
        )

    far = (4, 3, 5, 2, 6, 1, 7)

    def edge_up(pair):
        return send(
            ext.at[pl.ds(2 * pair, 2), 15], edge.at[0, pl.ds(2 * pair, 2)],
            d_send.at[pair, 0], d_recv.at[pair, 0], me_b, me_s + 4,
        )

    def edge_down(pair):
        return send(
            ext.at[pl.ds(2 * pair, 2), 8], edge.at[1, pl.ds(2 * pair, 2)],
            d_send.at[pair, 1], d_recv.at[pair, 1], me_b, me_s - 4,
        )

    for pair in range(2):
        for o in (2 * pair, 2 * pair + 1):

            @pl.when(low)
            def _():
                up(o).wait_recv()
                down(o).wait_send()

            @pl.when(high)
            def _():
                down(o).wait_recv()
                up(o).wait_send()

        for t, (scale, back) in enumerate(coefficients, 1):
            if t % 2 == 1:
                apply(ext, 2 * pair, work, 0, t, 24 - 2 * t, scale, back, 3.0 - centre, True)
            else:
                apply(work, 0, ext, 2 * pair, t, 24 - 2 * t, scale, back, 3.0 - centre, True)

        def rounded(p, carry):
            value = ext[pl.ds(2 * pair, 2), 8 + p].reshape(2 * NY, NZ).astype(BF16)
            fb[pair, p] = value
            ext[pl.ds(2 * pair, 2), 8 + p] = value.astype(F32).reshape(2, NY, NZ)
            return carry

        lax.fori_loop(0, 8, rounded, 0)

        @pl.when(high)
        def _():
            edge_up(pair).start()

        @pl.when(low)
        def _():
            edge_down(pair).start()

        for d in far:
            f_copy(pair, d).start()
        fr[z, pair] = fb[pair, z]

    for pair in range(2):

        @pl.when(low)
        def _():
            edge_up(pair).wait_recv()

        @pl.when(high)
        def _():
            edge_down(pair).wait_recv()

        ext[pl.ds(2 * pair, 2), 7] = edge[0, pl.ds(2 * pair, 2)]
        ext[pl.ds(2 * pair, 2), 16] = edge[1, pl.ds(2 * pair, 2)]
        apply(ext, 2 * pair, work, 0, 8, 8, 1.0, 0.0, 3.0, False)

        def stored(p, carry):
            hb[pair, p] = work[:, 8 + p].reshape(2 * NY, NZ).astype(BF16)
            return carry

        lax.fori_loop(0, 8, stored, 0)
        for d in far:
            h_copy(pair, d).start()
        hr[z, pair] = hb[pair, z]

    def turned(src, dst):
        value = src[...].reshape(Z * 4 * NY, NZ).astype(F32).reshape(Z * 4, NY, NZ)
        dst[...] = jnp.swapaxes(value, 0, 1).reshape(NY * Z * 4, NZ).astype(BF16).reshape(
            NY, Z * 4, NZ
        )

    for pair in range(2):
        for d in range(1, Z):
            f_copy(pair, d).wait_recv()
    turned(fr, f1)
    for pair in range(2):
        for d in range(1, Z):
            h_copy(pair, d).wait_recv()
    turned(hr, h1)

    for d in range(1, ZH):
        r_copy(d).wait()
    for o in range(4):
        for d in range(1, 4):
            a_copy(o, d).wait_send()
    v_mate.wait_send()
    v_core.wait_send()
    for pair in range(2):
        for d in range(1, Z):
            f_copy(pair, d).wait_send()
            h_copy(pair, d).wait_send()

    @pl.when(high)
    def _():
        v_up.wait_send()
        for pair in range(2):
            edge_up(pair).wait_send()

    @pl.when(low)
    def _():
        v_down.wait_send()
        for pair in range(2):
            edge_down(pair).wait_send()


def filtered_blocks(n_x, n_y, orbitals, potential, rt):
    dma = pltpu.SemaphoreType.DMA
    return pl.pallas_call(
        functools.partial(filter_kernel, n_x, n_y),
        out_shape=(
            jax.ShapeDtypeStruct((NY, 4 * Z, NZ), BF16),
            jax.ShapeDtypeStruct((NY, 4 * Z, NZ), BF16),
            jax.ShapeDtypeStruct((16 * ZH, rt.shape[1]), BF16),
        ),
        in_specs=[pl.BlockSpec(memory_space=VMEM)] * 3,
        out_specs=[pl.BlockSpec(memory_space=VMEM)] * 3,
        scratch_shapes=[
            VMEM((4, 24, NY, NZ), F32),
            VMEM((2, 24, NY, NZ), F32),
            VMEM((3, 2, 2, 2, NY, NZ), F32),
            VMEM((2, 4, NY, NZ), F32),
            VMEM((2, Z, 2 * NY, NZ), BF16),
            VMEM((2, Z, 2 * NY, NZ), BF16),
            VMEM((Z, 2, 2 * NY, NZ), BF16),
            VMEM((Z, 2, 2 * NY, NZ), BF16),
            dma((4, 3)), dma((4, 3)), dma((4, 2)), dma((4, 2)), dma((4,)), dma((4,)),
            dma((2, 2)), dma((2, 2)), dma((2, Z - 1)), dma((2, Z - 1)),
            dma((2, Z - 1)), dma((2, Z - 1)), dma((ZH - 1,)), dma((ZH - 1,)),
        ],
        compiler_params=pltpu.CompilerParams(
            collective_id=0, has_side_effects=True, vmem_limit_bytes=40 * 2**20
        ),
    )(orbitals, potential, rt)


def hops(n_x, chunk):
    right, left = n_x // 2, (n_x - 1) // 2
    return (left, right) if chunk % 2 == 1 else (right, left)


def product_kernel(
    n_x, n_y, f1, h1, rt_all, rotated, blocks,
    got, acc, rows, turned, part, summed, last,
    right_send, right_recv, left_send, left_recv, core_send, core_recv,
    back_send, back_recv, y_send, y_recv, z_send, z_recv, own_sem,
):
    zh, x, y, q, zl, c = position(n_x)
    z = zh * 2 + zl
    me_b, me_s = zh * n_x + x, y * 4 + q
    right_b = zh * n_x + lax.rem(x + 1, n_x)
    left_b = zh * n_x + lax.rem(x + n_x - 1, n_x)
    core = y * 4 + zl * 2 + (1 - c)

    barrier = pltpu.get_barrier_semaphore()

    def greet(band, space):
        pl.semaphore_signal(
            barrier, inc=1, device_id={"band": band, "space": space}, device_id_type=MESH
        )

    def along(e):
        other = lax.rem(z * 2 + c + e, 2 * Z)
        oz, oc = other // 2, lax.rem(other, 2)
        return oz, oc, (oz // 2) * n_x + x, y * 4 + lax.rem(oz, 2) * 2 + oc

    for e in range(1, 2 * Z):
        _, _, band, space = along(e)
        greet(band, space)
    for d in range(1, n_y):
        greet(me_b, lax.rem(y + d, n_y) * 4 + q)
    greet(right_b, me_s)
    greet(left_b, me_s)
    pl.semaphore_wait(barrier, 2 * Z - 1 + n_y - 1 + 2)

    def block(cls, owner, chunk):
        return got.at[cls, owner, pl.ds(chunk * ROWS, ROWS)]

    def go_right(hop, chunk):
        owner = lax.rem(x - hop + n_x, n_x)
        src = f1.at[pl.ds(chunk * ROWS, ROWS)] if hop == 0 else block(c, owner, chunk)
        return send(
            src, block(c, owner, chunk),
            right_send.at[hop, chunk], right_recv.at[hop, chunk], right_b, me_s,
        )

    def go_left(hop, chunk):
        owner = lax.rem(x + hop, n_x)
        src = f1.at[pl.ds(chunk * ROWS, ROWS)] if hop == 0 else block(c, owner, chunk)
        return send(
            src, block(c, owner, chunk),
            left_send.at[hop, chunk], left_recv.at[hop, chunk], left_b, me_s,
        )

    def go_core(slot, chunk):
        owner = lax.rem(x - slot + n_x, n_x)
        src = f1.at[pl.ds(chunk * ROWS, ROWS)] if slot == 0 else block(c, owner, chunk)
        return send(
            src, block(c, owner, chunk),
            core_send.at[slot, chunk], core_recv.at[slot, chunk], me_b, core,
        )

    for chunk in range(CHUNKS):
        n_right, n_left = hops(n_x, chunk)
        if n_right > 0:
            go_right(0, chunk).start()
        if n_left > 0:
            go_left(0, chunk).start()
    for chunk in range(CHUNKS):
        go_core(0, chunk).start()
    own = pltpu.make_async_copy(f1, got.at[c, x], own_sem)
    own.start()
    acc[...] = jnp.zeros_like(acc)
    own.wait()

    def chunk_products(chunk):
        zero = jnp.zeros((64, NZ), BF16)

        def body(k, carry):
            r = chunk * ROWS + k
            ours = jnp.concatenate([f1[r], h1[r]], axis=0)
            factor = jnp.concatenate(
                [
                    jnp.concatenate([ours, zero], axis=0),
                    jnp.concatenate([zero, ours], axis=0),
                ],
                axis=1,
            )
            zero_class = got[0, :, r].reshape(n_x * 32, NZ)
            one_class = got[1, :, r].reshape(n_x * 32, NZ)
            both = jnp.concatenate([zero_class, one_class], axis=1)
            acc[...] += lax.dot_general(
                both, factor, (((1,), (1,)), ((), ())), preferred_element_type=F32
            ).reshape(n_x, 32, NZ)
            every = jnp.concatenate([zero_class, one_class], axis=0)
            rows[k] = jnp.dot(
                rt_all[pl.ds(pl.multiple_of(32 * c, 32), 32)],
                every,
                preferred_element_type=F32,
            )
            return carry

        lax.fori_loop(0, ROWS, body, 0)
        turned[chunk] = jnp.swapaxes(rows[...], 0, 1).reshape(2, 16, ROWS, NZ)

    home_q = z // 2
    home_s = y * 4 + home_q

    def give_back(m, chunk):
        return send(
            turned.at[chunk, m],
            rotated.at[:, lax.rem(z, 2), pl.ds(chunk * ROWS, ROWS)],
            back_send.at[m, chunk], back_recv.at[lax.rem(z, 2), chunk],
            (2 * c + m) * n_x + x, home_s,
        )

    def keep(m, chunk):
        return pltpu.make_async_copy(
            turned.at[chunk, m],
            rotated.at[:, lax.rem(z, 2), pl.ds(chunk * ROWS, ROWS)],
            back_send.at[m, chunk],
        )

    def is_self(m):
        return (home_q == q) & (2 * c + m == zh)

    def come_back(plane, chunk):
        return send(
            turned.at[chunk, 0],
            rotated.at[:, plane, pl.ds(chunk * ROWS, ROWS)],
            back_send.at[0, chunk], back_recv.at[plane, chunk], me_b, core,
        )

    top = max(n_x // 2, 1)
    for hop in range(1, top + 1):
        for chunk in range(CHUNKS):
            n_right, n_left = hops(n_x, chunk)
            if hop <= n_right:
                go_right(hop - 1, chunk).wait_recv()
                if hop < n_right:
                    go_right(hop, chunk).start()
                go_core(hop, chunk).start()
            if hop <= n_left:
                go_left(hop - 1, chunk).wait_recv()
                if hop < n_left:
                    go_left(hop, chunk).start()
                go_core(n_x - hop, chunk).start()

    for chunk in range(CHUNKS):
        for slot in range(n_x):
            go_core(slot, chunk).wait_recv()
        chunk_products(chunk)
        for m in range(2):

            @pl.when(is_self(m))
            def _():
                keep(m, chunk).start()

            @pl.when(jnp.logical_not(is_self(m)))
            def _():
                give_back(m, chunk).start()

    def y_copy(d):
        to = lax.rem(y + d, n_y)
        first = 4 * to
        return send(
            acc.at[
                pl.ds(lax.rem(first, n_x), 4),
                pl.ds(pl.multiple_of(first // n_x * 8, 8), 8),
            ],
            part.at[y], y_send.at[d - 1], y_recv.at[d - 1], me_b, to * 4 + q,
        )

    for d in range(1, n_y):
        y_copy(d).start()
    mine = 4 * y
    part[y] = acc[
        pl.ds(lax.rem(mine, n_x), 4), pl.ds(pl.multiple_of(mine // n_x * 8, 8), 8)
    ]
    for d in range(1, n_y):
        y_copy(d).wait_recv()
    total = part[0]
    for k in range(1, n_y):
        total = total + part[k]
    summed[...] = total

    def z_copy(e):
        oz, oc, band, space = along(e)
        return send(
            summed.at[lax.rem(oz, 2) * 2 + oc], last.at[c, z],
            z_send.at[e - 1], z_recv.at[e - 1], band, space,
        )

    for e in range(1, 2 * Z):
        z_copy(e).start()
    last[c, z] = summed[q]
    for e in range(1, 2 * Z):
        z_copy(e).wait_recv()
    for cls in range(2):
        value = last[cls, 0]
        for k in range(1, Z):
            value = value + last[cls, k]
        blocks[cls] = value

    for plane in range(2):
        from_me = (2 * q + plane == z) & (c == zh // 2)
        for chunk in range(CHUNKS):

            @pl.when(jnp.logical_not(from_me))
            def _():
                come_back(plane, chunk).wait_recv()

    for m in range(2):

        @pl.when(is_self(m))
        def _():
            for chunk in range(CHUNKS):
                keep(m, chunk).wait()

        @pl.when(jnp.logical_not(is_self(m)))
        def _():
            for chunk in range(CHUNKS):
                give_back(m, chunk).wait_send()

    for chunk in range(CHUNKS):
        n_right, n_left = hops(n_x, chunk)
        for hop in range(n_right):
            go_right(hop, chunk).wait_send()
        for hop in range(n_left):
            go_left(hop, chunk).wait_send()
        for slot in range(n_x):
            go_core(slot, chunk).wait_send()
    for d in range(1, n_y):
        y_copy(d).wait_send()
    for e in range(1, 2 * Z):
        z_copy(e).wait_send()


def products(n_x, n_y, f1, h1, rt_all):
    dma = pltpu.SemaphoreType.DMA
    top = max(n_x // 2, 1)
    return pl.pallas_call(
        functools.partial(product_kernel, n_x, n_y),
        out_shape=(
            jax.ShapeDtypeStruct((16, 2, NY, NZ), F32),
            jax.ShapeDtypeStruct((2, 8, NZ), F32),
        ),
        in_specs=[pl.BlockSpec(memory_space=VMEM)] * 3,
        out_specs=[pl.BlockSpec(memory_space=VMEM)] * 2,
        scratch_shapes=[
            VMEM((2, n_x, NY, 32, NZ), BF16),
            VMEM((n_x, 32, NZ), F32),
            VMEM((ROWS, 32, NZ), F32),
            VMEM((CHUNKS, 2, 16, ROWS, NZ), F32),
            VMEM((n_y, 4, 8, NZ), F32),
            VMEM((4, 8, NZ), F32),
            VMEM((2, Z, 8, NZ), F32),
            dma((top, CHUNKS)), dma((top, CHUNKS)), dma((top, CHUNKS)), dma((top, CHUNKS)),
            dma((n_x, CHUNKS)), dma((n_x, CHUNKS)), dma((2, CHUNKS)), dma((2, CHUNKS)),
            dma((max(n_y - 1, 1),)), dma((max(n_y - 1, 1),)),
            dma((2 * Z - 1,)), dma((2 * Z - 1,)), dma(()),
        ],
        compiler_params=pltpu.CompilerParams(
            collective_id=1, has_side_effects=True, vmem_limit_bytes=40 * 2**20
        ),
    )(f1, h1, rt_all)


def shards(orbitals, potential, rotation):
    n_x = lax.axis_size("band") // ZH
    n_y = lax.axis_size("space") // 4
    cols = rotation.shape[1]
    rt = rotation.astype(BF16).reshape(ZH, n_x, 2, 2, 4, cols)
    rt = rt.transpose(5, 3, 1, 0, 2, 4).reshape(cols, -1)
    f1, h1, rt_all = filtered_blocks(n_x, n_y, orbitals, potential, rt)
    rotated, blocks = products(n_x, n_y, f1, h1, rt_all)
    blocks = blocks.reshape(2, 2, 4, 2, 2, ZH, 2, 4)
    blocks = lax.dynamic_index_in_dim(blocks, lax.axis_index("band") // n_x, 5, keepdims=False)
    blocks = blocks.transpose(4, 5, 0, 6, 1, 3, 2).reshape(2, 16, 16)
    return (blocks[0], blocks[1], rotated)


def solution(mesh):
    placed = (P("band", "space", None, None), P("space", None, None), P(None, "band"))
    return jax.shard_map(
        shards,
        mesh=mesh,
        in_specs=placed,
        out_specs=(P("band", "space"), P("band", "space"), P("band", "space", None, None)),
        check_vma=False,
    )
```

time: 469 us -> 103 us (0.22)
  waiting for transfers between devices: 370 us -> 0 us
  Pallas kernels: 0 us -> 97.1 us
  starting transfers between devices: 52.1 us -> 0 us
  between operations: 14.4 us -> 0.72 us
  matrix products: 10.9 us -> 0 us
  local copies, waits for them, and re-layouts: 13.2 us -> 4.73 us
  other arithmetic: 6.58 us -> 0 us
    psum x1 -> x0, waiting for transfers between devices: 190 us -> none  [shards(): summed = lax.psum(partials, 'space')]
    all_gather x1 -> x0, waiting for transfers between devices: 148 us -> none  [shards(): gathered = lax.all_gather(filtered_b, 'band', axis=0, tiled=True)]
    pallas_call x0 -> x2, Pallas kernels: none -> 97.1 us  [the longest x1 50.3 us: filtered_blocks(): pl.pallas_call(functools.partial(filter_kernel, n_x, n_y), out_shape=(jax...]
    ppermute x18 -> x0, starting transfers between devices: 52 us -> none  [the longest x9 30 us: extended(): after = lax.ppermute(leading, axis, down)]
    ppermute x18 -> x0, waiting for transfers between devices: 32.7 us -> none  [the longest x9 24.9 us: extended(): after = lax.ppermute(leading, axis, down)]
    dot_general x3 -> x0, matrix products: 10.9 us -> none  [the longest x2 6.37 us: contract_nodes(): lax.dot_general(left, right, (((1,), (1,)), ((), ())), preferred_element_...]
    all_gather x1 -> x0, local copies, waits for them, and re-layouts: 8.67 us -> none  [shards(): gathered = lax.all_gather(filtered_b, 'band', axis=0, tiled=True)]
  transfers between devices with their start and end apart: 20 -> 0, of which waited for: 17 -> 0; matrix products, arithmetic and copies ran while one was open for 4% -> 0% of each run, Pallas kernels for 0% -> 0%
where the time goes in v1:
time: 103 us; the launch traced here: 102 us
  Pallas kernels  97.1 us (94%)
  local copies, waits for them, and re-layouts  4.73 us (5%)
    pallas_call x1, Pallas kernels, filtered_blocks(): pl.pallas_call(functools.partial(filter_kernel, n_x, n_y), out_shape=(jax...  50.3 us
    pallas_call x1, Pallas kernels, products(): pl.pallas_call(functools.partial(product_kernel, n_x, n_y), out_shape=(ja...  46.8 us
    unnamed x6, local copies, waits for them, and re-layouts  2.33 us

profile of v1, /device:TPU:1, one launch (start us, length us, event | category | flops | bytes accessed | tf_op | source)
XLA Modules:
  0.0 102.5 jit_solution(6158959496855531695)
XLA Ops:
  0.6 0.0 copy-start
  0.6 0.9 copy.11
  1.6 0.0 copy-start.1
  1.6 0.1 copy.13.rt
  1.7 0.0 copy-done
  1.7 0.7 copy-done.1
  2.4 50.3 %shard_map.58 = (bf16[24,32,128]{2,1,0:T(8,128)(2,1)S(1)}, bf16[24,32,128]{2,1,0:T(8,128)(2,1)S(1)}, bf16[64,512]{1,0:T(8,128)(2,1)S(1)}) custom-call(f32[16,2,24,128]{3,2,1,0:T(8,128)S(1)} %copy-done, f32[2,24,128]{2,1,0:T(8,128)S(1)} %copy-done.1, bf16[16,512]{1,0:T(8,128)(2,1)S(1)} %copy.13.rt), custom_call_target="tpu_custom_call" | custom-call | tf_op jit(solution)/shard_map/pallas_call | solution.py:364
  52.7 46.8 %shard_map.59 = (f32[16,2,24,128]{3,2,1,0:T(8,128)S(1)}, f32[2,8,128]{2,1,0:T(8,128)S(1)}) custom-call(bf16[24,32,128]{2,1,0:T(8,128)(2,1)S(1)} %get-tuple-element.8.f1, bf16[24,32,128]{2,1,0:T(8,128)(2,1)S(1)} %get-tuple-element.9.h1, bf16[64,512]{1,0:T(8,128)(2,1)S(1)} %get-tuple-element.10.rt_all), custom_call_target="tpu_custom_call" | custom-call | tf_op jit(solution)/shard_map/pallas_call | solution.py:637
  99.4 0.4 reshape.22
  99.9 0.2 copy.15
  100.2 0.7 squeeze.11
  100.8 0.2 copy.16
  101.1 0.7 squeeze.12
  101.8 0.7 copy.19
  (3 shorter events, 0.1 us)
Async XLA Ops:
  0.6 1.1 %copy-start = (f32[16,2,24,128]{3,2,1,0:T(8,128)S(1)}, f32[16,2,24,128]{3,2,1,0:T(8,128)}, u32[]{:S(2)}) copy-start(f32[16,2,24,128]{3,2,1,0:T(8,128)} %orb.1) | copy-start | bytes 1179652
  1.6 0.7 copy-start.1

commit v2 on v0

v2 whole, which is shorter than its diff:
```python
import jax
import jax.numpy as jnp
from jax import lax
from jax.experimental import pallas as pl
from jax.experimental.pallas import tpu as pltpu
from jax.sharding import PartitionSpec as P

DEGREE = 8
FILTER_LOW = 2.0
FILTER_HIGH = 8.0
LOWER_EDGE = 0.0
MESH = pl.DeviceIdType.MESH
VMEM = pltpu.VMEM
F32 = jnp.float32
BF16 = jnp.bfloat16

ZH = 4
Z = 8
NY = 24
NZ = 128
PAD = 8
TALL = NY + 2 * PAD
DATA = slice(PAD, PAD + NY)
ROWS = 8
PIECES = ((0, 0, NY), (1, 0, ROWS), (1, ROWS, ROWS), (1, 2 * ROWS, ROWS))
CHUNKS = NY // ROWS


def steps():
    half_width = (FILTER_HIGH - FILTER_LOW) / 2.0
    centre = (FILTER_HIGH + FILTER_LOW) / 2.0
    first = half_width / (LOWER_EDGE - centre)
    ratio = first
    out = [(first / half_width, 0.0)]
    for _ in range(DEGREE - 1):
        ratio_next = 1.0 / (2.0 / first - ratio)
        out.append((2.0 * ratio_next / half_width, ratio * ratio_next))
        ratio = ratio_next
    return centre, out


def hops(n_x, pair):
    right, left = n_x // 2, (n_x - 1) // 2
    return (left, right) if pair == 1 else (right, left)


def send(src, dst, send_sem, recv_sem, band, space):
    return pltpu.make_async_remote_copy(
        src_ref=src,
        dst_ref=dst,
        send_sem=send_sem,
        recv_sem=recv_sem,
        device_id={"band": band, "space": space},
        device_id_type=MESH,
    )


def whole_kernel(
    n_x, n_y, orb, pot, rotation_in, gram, projected, rotated,
    rotation, own_sem, ext, work, pv, edge, rt_all, fb, hb, fr, hr, h_own,
    got, acc, acc_sent, rot, rows, back_out, back_in, part, summed, last,
    a_send, a_recv, b_send, b_recv, v_send, v_recv, d_send, d_recv,
    f_send, f_recv, h_send, h_recv, r_send, r_recv,
    right_send, right_recv, left_send, left_recv, core_send, core_recv,
    back_send, back_recv, y_send, y_recv, z_send, z_recv,
):
    bi, si = lax.axis_index("band"), lax.axis_index("space")
    zh, x = bi // n_x, lax.rem(bi, n_x)
    y, q = si // 4, lax.rem(si, 4)
    zl, c = q // 2, lax.rem(q, 2)
    z = zh * 2 + zl
    low, high = y > 0, y < n_y - 1
    right_b = zh * n_x + lax.rem(x + 1, n_x)
    left_b = zh * n_x + lax.rem(x + n_x - 1, n_x)
    mate = y * 4 + (1 - zl) * 2 + c
    core = y * 4 + zl * 2 + (1 - c)

    def along(e):
        other = lax.rem(z * 2 + c + e, 2 * Z)
        oz, oc = other // 2, lax.rem(other, 2)
        return oz, oc, (oz // 2) * n_x + x, y * 4 + lax.rem(oz, 2) * 2 + oc

    def along_z(d):
        other = lax.rem(z + d, Z)
        return other, (other // 2) * n_x + x, y * 4 + lax.rem(other, 2) * 2 + c

    barrier = pltpu.get_barrier_semaphore()

    def greet(band, space):
        pl.semaphore_signal(
            barrier, inc=1, device_id={"band": band, "space": space}, device_id_type=MESH
        )

    for e in range(1, 2 * Z):
        _, _, band, space = along(e)
        greet(band, space)
    for d in range(1, n_y):
        greet(bi, lax.rem(y + d, n_y) * 4 + q)
    greet(right_b, si)
    greet(left_b, si)

    blank = jnp.zeros((PAD, NZ), F32)

    def clear(p, carry):
        for o in range(4):
            ext[o, p, 0:PAD] = blank
            ext[o, p, PAD + NY : TALL] = blank
        for o in range(2):
            work[o, p, 0:PAD] = blank
            work[o, p, PAD + NY : TALL] = blank
        return carry

    lax.fori_loop(0, 24, clear, 0)

    def empty(first, slab, side):
        def body(p, carry):
            for o in range(4):
                ext[o, first + p, DATA] = jnp.zeros((NY, NZ), F32)
            return carry

        lax.fori_loop(0, 8, body, 0)
        pv[slab] = jnp.zeros((2, 2, 2, NY, NZ), F32)
        edge[side] = jnp.zeros((4, NY, NZ), F32)

    @pl.when(y == 0)
    def _():
        empty(0, 0, 0)

    @pl.when(y == n_y - 1)
    def _():
        empty(16, 2, 1)

    pl.semaphore_wait(barrier, 2 * Z - 1 + n_y - 1 + 2)

    v_mate = send(pot, pv.at[1, zl, c], v_send.at[0], v_recv.at[0], bi, mate)
    v_mate.start()

    def partner(d):
        return (1 - zl if d >= 2 else zl) * 2 + (1 - c if d % 2 else c)

    def pair_of(p):
        return slice(2 * p, 2 * p + 2)

    def a_copy(p, d):
        to = partner(d)
        return send(
            orb.at[pl.ds(4 * to + 2 * p, 2)], ext.at[pair_of(p), pl.ds(8 + 2 * q, 2), DATA],
            a_send.at[p, d - 1], a_recv.at[p, d - 1], bi, y * 4 + to,
        )

    def a_wait(p, d):
        of = partner(d)
        send(
            orb.at[pl.ds(4 * q + 2 * p, 2)], ext.at[pair_of(p), pl.ds(8 + 2 * of, 2), DATA],
            a_send.at[p, d - 1], a_recv.at[p, d - 1], bi, y * 4 + of,
        ).wait_recv()

    def own_copy(p):
        return pltpu.make_async_copy(
            orb.at[pl.ds(4 * q + 2 * p, 2)], ext.at[pair_of(p), pl.ds(8 + 2 * q, 2), DATA],
            own_sem.at[p],
        )

    def b_copy(p, d, side):
        of = partner(d)
        here = ext.at[pair_of(p), pl.ds(8 + 2 * of, 2), DATA]
        if d == 0:
            here = orb.at[pl.ds(4 * q + 2 * p, 2)]
        return send(
            here, ext.at[pair_of(p), pl.ds(16 * side + 2 * of, 2), DATA],
            b_send.at[p, d, side], b_recv.at[p, d, side], bi, si + 4 - 8 * side,
        )

    def pass_on(p, d):
        @pl.when(high)
        def _():
            b_copy(p, d, 0).start()

        @pl.when(low)
        def _():
            b_copy(p, d, 1).start()

    for p in range(2):
        for d in (2, 1, 3):
            a_copy(p, d).start()
        if p == 0:
            pass_on(0, 0)
    load_pot = pltpu.make_async_copy(pot, pv.at[1, zl, c], own_sem.at[2])
    load_pot.start()
    load_rotation = pltpu.make_async_copy(rotation_in, rotation, own_sem.at[3])
    load_rotation.start()
    for p in range(2):
        own_copy(p).start()

    v_up = send(pv.at[1, :, c], pv.at[0, :, c], v_send.at[1], v_recv.at[1], bi, si + 4)
    v_down = send(pv.at[1, :, c], pv.at[2, :, c], v_send.at[2], v_recv.at[2], bi, si - 4)

    a_wait(0, 1)
    pass_on(0, 1)
    load_pot.wait()
    v_mate.wait_recv()

    @pl.when(high)
    def _():
        v_up.start()

    @pl.when(low)
    def _():
        v_down.start()

    a_wait(0, 2)
    pass_on(0, 2)
    a_wait(0, 3)
    pass_on(0, 3)
    pass_on(1, 0)
    for d in (1, 2, 3):
        a_wait(1, d)
        pass_on(1, d)
    load_rotation.wait()
    for p in range(2):
        own_copy(p).wait()

    count = rotation.shape[1]
    i = lax.broadcasted_iota(jnp.int32, (count, count), 0)
    k = lax.broadcasted_iota(jnp.int32, (count, count), 1)
    half = n_x * 16
    source = (
        16 * (((k // 4) % 4) * n_x + (k // 16) % n_x)
        + 8 * ((k // 2) % 2)
        + 4 * ((k // half) % 2)
        + 2 * (k // (2 * half))
        + k % 2
    )
    order = jnp.where(i == source, 1.0, 0.0).astype(BF16)
    my_rt = pl.ds(pl.multiple_of(16 * zh, 16), 16)
    rt_all[my_rt] = lax.dot_general(
        rotation[...].astype(BF16), order, (((1,), (0,)), ((), ())), preferred_element_type=F32
    ).astype(BF16)

    def r_copy(d):
        to = lax.rem(zh + d, ZH)
        return send(
            rt_all.at[my_rt], rt_all.at[my_rt],
            r_send.at[d - 1], r_recv.at[d - 1], to * n_x + x, si,
        )

    def r_wait(d):
        of = lax.rem(zh + ZH - d, ZH)
        theirs = rt_all.at[pl.ds(pl.multiple_of(16 * of, 16), 16)]
        send(theirs, theirs, r_send.at[d - 1], r_recv.at[d - 1], of * n_x + x, si).wait_recv()

    for d in range(1, ZH):
        r_copy(d).start()

    @pl.when(low)
    def _():
        v_up.wait_recv()

    @pl.when(high)
    def _():
        v_down.wait_recv()

    v_core = send(pv.at[:, :, c], pv.at[:, :, c], v_send.at[3], v_recv.at[3], bi, core)
    v_core.start()
    send(
        pv.at[:, :, 1 - c], pv.at[:, :, 1 - c], v_send.at[3], v_recv.at[3], bi, core
    ).wait_recv()

    centre, coefficients = steps()
    lane = lax.broadcasted_iota(jnp.int32, (1, NZ), 1)

    def potential(p):
        return pv[p // 8, lax.rem(p, 8) // 4, lax.rem(p, 4) // 2, lax.rem(p, 2)]

    def planes(src, s0, dst, d0, p, width, scale, back, shift):
        old = dst[pl.ds(d0, 2), pl.ds(p, width), DATA] if back != 0.0 else None
        mid = src[pl.ds(s0, 2), pl.ds(p - 1, width + 2), DATA]
        above = src[pl.ds(s0, 2), pl.ds(p, width), PAD - 1 : PAD + NY - 1]
        below = src[pl.ds(s0, 2), pl.ds(p, width), PAD + 1 : PAD + NY + 1]
        for k in range(width):
            now = mid[:, k + 1]
            flat = now.reshape(2 * NY, NZ)
            left = jnp.where(lane == 0, 0.0, pltpu.roll(flat, 1, 1))
            right = jnp.where(lane == NZ - 1, 0.0, pltpu.roll(flat, NZ - 1, 1))
            near = (left + right).reshape(2, NY, NZ)
            near = near + ((above[:, k] + below[:, k]) + (mid[:, k] + mid[:, k + 2]))
            level = (potential(p + k) + shift) * scale
            new = near * (-0.5 * scale) + level[None] * now
            if back != 0.0:
                new = new - back * old[:, k]
            dst[pl.ds(d0, 2), p + k, DATA] = new

    def apply(src, s0, dst, d0, first, count, scale, back, shift):
        def body(i, carry):
            planes(src, s0, dst, d0, first + 4 * i, 4, scale, back, shift)
            return carry

        lax.fori_loop(0, count // 4, body, 0)
        if count % 4:
            planes(src, s0, dst, d0, first + count - 2, 2, scale, back, shift)

    def f_copy(pair, d):
        other, band, space = along_z(d)
        return send(
            fb.at[pair, other], fr.at[z, pair],
            f_send.at[pair, d - 1], f_recv.at[pair, d - 1], band, space,
        )

    def h_copy(pair, d):
        other, band, space = along_z(d)
        return send(
            hb.at[pair, other], hr.at[z, pair],
            h_send.at[pair, d - 1], h_recv.at[pair, d - 1], band, space,
        )

    far = (4, 3, 5, 2, 6, 1, 7)

    def edge_up(pair):
        return send(
            ext.at[pl.ds(2 * pair, 2), 15, DATA], edge.at[0, pl.ds(2 * pair, 2)],
            d_send.at[pair, 0], d_recv.at[pair, 0], bi, si + 4,
        )

    def edge_down(pair):
        return send(
            ext.at[pl.ds(2 * pair, 2), 8, DATA], edge.at[1, pl.ds(2 * pair, 2)],
            d_send.at[pair, 1], d_recv.at[pair, 1], bi, si - 4,
        )

    def filtered(pair):
        for d in range(4):

            @pl.when(low)
            def _():
                b_copy(pair, d, 0).wait_recv()
                b_copy(pair, d, 1).wait_send()

            @pl.when(high)
            def _():
                b_copy(pair, d, 1).wait_recv()
                b_copy(pair, d, 0).wait_send()

        for t, (scale, back) in enumerate(coefficients, 1):
            src, s0, dst, d0 = (ext, 2 * pair, work, 0) if t % 2 else (work, 0, ext, 2 * pair)
            apply(src, s0, dst, d0, t, 24 - 2 * t, scale, back, 3.0 - centre)
            if t < DEGREE:

                @pl.when(y == 0)
                def _():
                    dst[pl.ds(d0, 2), 7, DATA] = jnp.zeros((2, NY, NZ), F32)

                @pl.when(y == n_y - 1)
                def _():
                    dst[pl.ds(d0, 2), 16, DATA] = jnp.zeros((2, NY, NZ), F32)

        def rounded(p, carry):
            value = ext[pl.ds(2 * pair, 2), 8 + p, DATA].reshape(2 * NY, NZ).astype(BF16)
            fb[pair, p] = value
            ext[pl.ds(2 * pair, 2), 8 + p, DATA] = value.astype(F32).reshape(2, NY, NZ)
            return carry

        lax.fori_loop(0, 8, rounded, 0)
        for d in far:
            f_copy(pair, d).start()
        fr[z, pair] = fb[pair, z]

        @pl.when(high)
        def _():
            edge_up(pair).start()

        @pl.when(low)
        def _():
            edge_down(pair).start()

    def turn(src, pair):
        value = src[:, pair].reshape(Z * 2 * NY, NZ).astype(F32).reshape(Z * 2, NY, NZ)
        value = jnp.swapaxes(value, 0, 1).reshape(NY * Z * 2, NZ).astype(BF16)
        return value.reshape(NY, Z * 2, NZ)

    def block(cls, owner, piece):
        pair, first, size = PIECES[piece]
        return got.at[cls, owner, pair, pl.ds(first, size)]

    def go_right(hop, piece):
        owner = lax.rem(x - hop + n_x, n_x)
        return send(
            block(c, owner, piece), block(c, owner, piece),
            right_send.at[hop, piece], right_recv.at[hop, piece], right_b, si,
        )

    def from_left(hop, piece):
        owner = lax.rem(x - hop - 1 + n_x, n_x)
        return send(
            block(c, owner, piece), block(c, owner, piece),
            right_send.at[hop, piece], right_recv.at[hop, piece], right_b, si,
        )

    def go_left(hop, piece):
        owner = lax.rem(x + hop, n_x)
        return send(
            block(c, owner, piece), block(c, owner, piece),
            left_send.at[hop, piece], left_recv.at[hop, piece], left_b, si,
        )

    def from_right(hop, piece):
        owner = lax.rem(x + hop + 1, n_x)
        return send(
            block(c, owner, piece), block(c, owner, piece),
            left_send.at[hop, piece], left_recv.at[hop, piece], left_b, si,
        )

    def go_core(slot, piece):
        owner = lax.rem(x - slot + n_x, n_x)
        return send(
            block(c, owner, piece), block(c, owner, piece),
            core_send.at[slot, piece], core_recv.at[slot, piece], bi, core,
        )

    def from_core(slot, piece):
        owner = lax.rem(x - slot + n_x, n_x)
        return send(
            block(1 - c, owner, piece), block(1 - c, owner, piece),
            core_send.at[slot, piece], core_recv.at[slot, piece], bi, core,
        )

    def launch(pair):
        for d in range(1, Z):
            f_copy(pair, d).wait_recv()
        got[c, x, pair] = turn(fr, pair)
        n_right, n_left = hops(n_x, pair)
        mine = [k for k in range(len(PIECES)) if PIECES[k][0] == pair]
        for piece in mine:
            if n_right > 0:
                go_right(0, piece).start()
            if n_left > 0:
                go_left(0, piece).start()
        for piece in mine:
            go_core(0, piece).start()

    def serve(hop, piece):
        n_right, n_left = hops(n_x, PIECES[piece][0])
        if hop <= n_right:
            from_left(hop - 1, piece).wait_recv()
            if hop < n_right:
                go_right(hop, piece).start()
            go_core(hop, piece).start()
        if hop <= n_left:
            from_right(hop - 1, piece).wait_recv()
            if hop < n_left:
                go_left(hop, piece).start()
            go_core(n_x - hop, piece).start()

    def applied(pair):
        @pl.when(low)
        def _():
            edge_up(pair).wait_recv()

        @pl.when(high)
        def _():
            edge_down(pair).wait_recv()

        ext[pl.ds(2 * pair, 2), 7, DATA] = edge[0, pl.ds(2 * pair, 2)]
        ext[pl.ds(2 * pair, 2), 16, DATA] = edge[1, pl.ds(2 * pair, 2)]
        apply(ext, 2 * pair, work, 0, 8, 8, 1.0, 0.0, 3.0)

        def stored(p, carry):
            hb[pair, p] = work[:, 8 + p, DATA].reshape(2 * NY, NZ).astype(BF16)
            return carry

        lax.fori_loop(0, 8, stored, 0)
        for d in far:
            h_copy(pair, d).start()
        hr[z, pair] = hb[pair, z]

    def take_applied(pair):
        for d in range(1, Z):
            h_copy(pair, d).wait_recv()
        h_own[pair] = turn(hr, pair)

    def take_core(piece):
        for slot in range(n_x):
            from_core(slot, piece).wait_recv()

    zero = jnp.zeros((4 * 16, NZ), BF16)

    def correlate(piece):
        pair, first, size = PIECES[piece]

        def body(g, carry):
            total = None
            for k in range(ROWS):
                r = first + g * ROWS + k
                ours = jnp.concatenate(
                    [got[c, x, 0, r], got[c, x, 1, r], h_own[0, r], h_own[1, r]], axis=0
                )
                factor = jnp.concatenate(
                    [
                        jnp.concatenate([ours, zero], axis=0),
                        jnp.concatenate([zero, ours], axis=0),
                    ],
                    axis=1,
                )
                both = jnp.concatenate(
                    [got[cls, :, pair, r].reshape(n_x * 16, NZ) for cls in range(2)], axis=1
                )
                value = lax.dot_general(
                    both, factor, (((1,), (1,)), ((), ())), preferred_element_type=F32
                )
                total = value if total is None else total + value
            acc[pair] += total.reshape(n_x, 16, NZ)
            return carry

        lax.fori_loop(0, size // ROWS, body, 0)

    my_rows = pl.ds(pl.multiple_of(32 * c, 32), 32)

    def rotate(piece):
        pair, first, size = PIECES[piece]

        ours = rt_all[my_rows, pair * 2 * half : (pair + 1) * 2 * half]

        def body(g, carry):
            for k in range(ROWS):
                r = first + g * ROWS + k
                every = got[:, :, pair, r].reshape(2 * n_x * 16, NZ)
                value = jnp.dot(ours, every, preferred_element_type=F32)
                if pair == 0:
                    rot[r] = value
                else:
                    rows[k] = rot[r] + value
            return carry

        lax.fori_loop(0, size // ROWS, body, 0)

    home_q = z // 2

    def is_self(m):
        return (home_q == q) & (2 * c + m == zh)

    def give_back(m, chunk):
        return send(
            back_out.at[chunk, m], back_in.at[lax.rem(z, 2), chunk],
            back_send.at[m, chunk], back_recv.at[lax.rem(z, 2), chunk],
            (2 * c + m) * n_x + x, y * 4 + home_q,
        )

    def come_back(plane, chunk):
        return send(
            back_out.at[chunk, 0], back_in.at[plane, chunk],
            back_send.at[0, chunk], back_recv.at[plane, chunk], bi, core,
        )

    def return_rows(chunk):
        value = jnp.swapaxes(rows[...], 0, 1).reshape(2, 16 * ROWS, NZ).astype(BF16)
        back_out[chunk] = value
        for m in range(2):

            @pl.when(is_self(m))
            def _():
                back_in[lax.rem(z, 2), chunk] = back_out[chunk, m]

            @pl.when(jnp.logical_not(is_self(m)))
            def _():
                give_back(m, chunk).start()

    acc[...] = jnp.zeros_like(acc)
    pieces = len(PIECES)
    filtered(0)
    launch(0)
    filtered(1)
    later = range(1, pieces)

    def serve_later(hop):
        for piece in later:
            serve(hop, piece)

    serve(1, 0)
    applied(0)
    serve(2, 0)
    launch(1)
    applied(1)
    serve(3, 0)
    serve_later(1)
    take_applied(0)
    serve(4, 0)
    serve_later(2)
    take_applied(1)
    for d in range(1, ZH):
        r_wait(d)
    take_core(0)
    rotate(0)
    serve_later(3)
    correlate(0)
    serve_later(4)
    for piece in range(1, pieces):
        take_core(piece)
        if piece == pieces - 1:
            break
        rotate(piece)
        return_rows(piece - 1)
        correlate(piece)
    correlate(pieces - 1)

    for pair in range(2):
        for k in range(ZH):
            acc_sent[:, 8 * k + 4 * pair : 8 * k + 4 * pair + 4] = acc[pair, :, 4 * k : 4 * k + 4]

    def columns_of(to):
        first = 4 * to
        return (
            pl.ds(lax.rem(first, n_x), 4),
            pl.ds(pl.multiple_of(first // n_x * 8, 8), 8),
        )

    def y_copy(d):
        to = lax.rem(y + d, n_y)
        return send(
            acc_sent.at[columns_of(to)], part.at[y],
            y_send.at[d - 1], y_recv.at[d - 1], bi, to * 4 + q,
        )

    for d in range(1, n_y):
        y_copy(d).start()
    part[y] = acc_sent[columns_of(y)]
    rotate(pieces - 1)
    return_rows(CHUNKS - 1)
    for d in range(1, n_y):
        y_copy(d).wait_recv()
    total = part[0]
    for k in range(1, n_y):
        total = total + part[k]
    summed[...] = total

    def z_copy(e):
        oz, oc, band, space = along(e)
        return send(
            summed.at[lax.rem(oz, 2) * 2 + oc], last.at[c, z],
            z_send.at[e - 1], z_recv.at[e - 1], band, space,
        )

    for e in range(1, 2 * Z):
        z_copy(e).start()
    last[c, z] = summed[q]

    for chunk in range(CHUNKS):
        for plane in range(2):
            from_me = (2 * q + plane == z) & (c == zh // 2)

            @pl.when(jnp.logical_not(from_me))
            def _():
                come_back(plane, chunk).wait_recv()

            rotated[:, plane, chunk * ROWS : (chunk + 1) * ROWS] = (
                back_in[plane, chunk].astype(F32).reshape(16, ROWS, NZ)
            )

    for e in range(1, 2 * Z):
        z_copy(e).wait_recv()
    n = lax.broadcasted_iota(jnp.int32, (64, NZ), 0)
    l = lax.broadcasted_iota(jnp.int32, (64, NZ), 1)
    lane_of = (
        64 * ((n // 16) % 2) + 32 * (n // 32)
        + 16 * ((n // 2) % 2) + 4 * zh + 2 * ((n // 8) % 2) + n % 2
    )
    picked = None
    for cls in range(2):
        value = last[cls, 0]
        for k in range(1, Z):
            value = value + last[cls, k]
        select = jnp.where((l == lane_of) & ((n // 4) % 2 == cls), 1.0, 0.0)
        value = lax.dot_general(
            select, value, (((1,), (1,)), ((), ())),
            precision=lax.Precision.HIGHEST, preferred_element_type=F32,
        )
        picked = value if picked is None else picked + value
    r = lax.broadcasted_iota(jnp.int32, (8, 16), 0)
    i = lax.broadcasted_iota(jnp.int32, (8, 16), 1)
    for side, out in enumerate((gram, projected)):
        value = None
        for cls in range(2):
            select = jnp.where(
                i == 8 * ((r // 2) % 2) + 4 * cls + 2 * (r // 4) + r % 2, 1.0, 0.0
            )
            first = 32 * side + 16 * cls
            term = jnp.dot(
                picked[first : first + 16], select,
                precision=lax.Precision.HIGHEST, preferred_element_type=F32,
            )
            value = term if value is None else value + term
        out[...] = value

    for d in range(1, ZH):
        r_copy(d).wait_send()
    for p in range(2):
        for d in range(1, 4):
            a_copy(p, d).wait_send()
    v_mate.wait_send()
    v_core.wait_send()
    for pair in range(2):
        for d in range(1, Z):
            f_copy(pair, d).wait_send()
            h_copy(pair, d).wait_send()

    @pl.when(high)
    def _():
        v_up.wait_send()
        for pair in range(2):
            edge_up(pair).wait_send()

    @pl.when(low)
    def _():
        v_down.wait_send()
        for pair in range(2):
            edge_down(pair).wait_send()

    for piece in range(pieces):
        n_right, n_left = hops(n_x, PIECES[piece][0])
        for hop in range(n_right):
            go_right(hop, piece).wait_send()
        for hop in range(n_left):
            go_left(hop, piece).wait_send()
        for slot in range(n_x):
            go_core(slot, piece).wait_send()
    for chunk in range(CHUNKS):
        for m in range(2):

            @pl.when(jnp.logical_not(is_self(m)))
            def _():
                give_back(m, chunk).wait_send()

    for d in range(1, n_y):
        y_copy(d).wait_send()
    for e in range(1, 2 * Z):
        z_copy(e).wait_send()


def shards(orbitals, potential, rotation):
    n_x = lax.axis_size("band") // ZH
    n_y = lax.axis_size("space") // 4
    top, pieces = max(n_x // 2, 1), len(PIECES)
    dma = pltpu.SemaphoreType.DMA

    def kernel(*refs):
        whole_kernel(n_x, n_y, *refs)

    return pl.pallas_call(
        kernel,
        out_shape=(
            jax.ShapeDtypeStruct((16, 16), F32),
            jax.ShapeDtypeStruct((16, 16), F32),
            jax.ShapeDtypeStruct(orbitals.shape, F32),
        ),
        in_specs=[pl.BlockSpec(memory_space=pltpu.HBM)] * 3,
        out_specs=[pl.BlockSpec(memory_space=VMEM)] * 3,
        scratch_shapes=[
            VMEM(rotation.shape[::-1], F32), dma((4,)),
            VMEM((4, 24, TALL, NZ), F32),
            VMEM((2, 24, TALL, NZ), F32),
            VMEM((3, 2, 2, 2, NY, NZ), F32),
            VMEM((2, 4, NY, NZ), F32),
            VMEM((16 * ZH, rotation.shape[0]), BF16),
            VMEM((2, Z, 2 * NY, NZ), BF16),
            VMEM((2, Z, 2 * NY, NZ), BF16),
            VMEM((Z, 2, 2 * NY, NZ), BF16),
            VMEM((Z, 2, 2 * NY, NZ), BF16),
            VMEM((2, NY, 2 * Z, NZ), BF16),
            VMEM((2, n_x, 2, NY, 2 * Z, NZ), BF16),
            VMEM((2, n_x, 2 * Z, NZ), F32),
            VMEM((n_x, 4 * Z, NZ), F32),
            VMEM((NY, 32, NZ), F32),
            VMEM((ROWS, 32, NZ), F32),
            VMEM((CHUNKS, 2, 16 * ROWS, NZ), BF16),
            VMEM((2, CHUNKS, 16 * ROWS, NZ), BF16),
            VMEM((n_y, 4, 8, NZ), F32),
            VMEM((4, 8, NZ), F32),
            VMEM((2, Z, 8, NZ), F32),
            dma((2, 3)), dma((2, 3)), dma((2, 4, 2)), dma((2, 4, 2)), dma((4,)), dma((4,)),
            dma((2, 2)), dma((2, 2)), dma((2, Z - 1)), dma((2, Z - 1)),
            dma((2, Z - 1)), dma((2, Z - 1)), dma((ZH - 1,)), dma((ZH - 1,)),
            dma((top, pieces)), dma((top, pieces)), dma((top, pieces)), dma((top, pieces)),
            dma((n_x, pieces)), dma((n_x, pieces)), dma((2, CHUNKS)), dma((2, CHUNKS)),
            dma((n_y - 1,)), dma((n_y - 1,)), dma((2 * Z - 1,)), dma((2 * Z - 1,)),
        ],
        compiler_params=pltpu.CompilerParams(
            collective_id=0, has_side_effects=True, vmem_limit_bytes=60 * 2**20
        ),
    )(orbitals, potential, rotation.T)


def solution(mesh):
    placed = (P("band", "space", None, None), P("space", None, None), P(None, "band"))
    return jax.shard_map(
        shards,
        mesh=mesh,
        in_specs=placed,
        out_specs=(P("band", "space"), P("band", "space"), P("band", "space", None, None)),
        check_vma=False,
    )
```

time: 469 us -> 86.3 us (0.18)
  waiting for transfers between devices: 370 us -> 0 us
  Pallas kernels: 0 us -> 81.7 us
  starting transfers between devices: 52.1 us -> 0 us
  between operations: 14.4 us -> 0.65 us
  matrix products: 10.9 us -> 0 us
  local copies, waits for them, and re-layouts: 13.2 us -> 3.67 us
  other arithmetic: 6.58 us -> 0 us
    psum x1 -> x0, waiting for transfers between devices: 190 us -> none  [shards(): summed = lax.psum(partials, 'space')]
    all_gather x1 -> x0, waiting for transfers between devices: 148 us -> none  [shards(): gathered = lax.all_gather(filtered_b, 'band', axis=0, tiled=True)]
    pallas_call x0 -> x1, Pallas kernels: none -> 81.7 us  [shards(): pl.pallas_call(kernel, out_shape=(jax.ShapeDtypeStruct((16, 16), F32), ja...]
    ppermute x18 -> x0, starting transfers between devices: 52 us -> none  [the longest x9 30 us: extended(): after = lax.ppermute(leading, axis, down)]
    ppermute x18 -> x0, waiting for transfers between devices: 32.7 us -> none  [the longest x9 24.9 us: extended(): after = lax.ppermute(leading, axis, down)]
    dot_general x3 -> x0, matrix products: 10.9 us -> none  [the longest x2 6.37 us: contract_nodes(): lax.dot_general(left, right, (((1,), (1,)), ((), ())), preferred_element_...]
    all_gather x1 -> x0, local copies, waits for them, and re-layouts: 8.67 us -> none  [shards(): gathered = lax.all_gather(filtered_b, 'band', axis=0, tiled=True)]
  transfers between devices with their start and end apart: 20 -> 0, of which waited for: 17 -> 0; matrix products, arithmetic and copies ran while one was open for 4% -> 0% of each run, Pallas kernels for 0% -> 0%
where the time goes in v2:
time: 86.3 us; the launch traced here: 86 us
  Pallas kernels  81.7 us (95%)
  local copies, waits for them, and re-layouts  3.67 us (4%)
    pallas_call x1, Pallas kernels, shards(): pl.pallas_call(kernel, out_shape=(jax.ShapeDtypeStruct((16, 16), F32), ja...  81.7 us
    unnamed x5, local copies, waits for them, and re-layouts  3.67 us

profile of v2, /device:TPU:1, one launch (start us, length us, event | category | flops | bytes accessed | tf_op | source)
XLA Modules:
  0.0 86.0 jit_solution(326671008354517909)
XLA Ops:
  0.6 81.7 %shard_map.58 = (f32[16,16]{1,0:T(8,128)}, f32[16,16]{1,0:T(8,128)}, f32[16,2,24,128]{3,2,1,0:T(8,128)}) custom-call(f32[16,2,24,128]{3,2,1,0:T(8,128)} %refs_0_.1, f32[2,24,128]{2,1,0:T(8,128)} %refs_1_.1, f32[16,512]{1,0:T(8,128)} %bitcast.1), custom_call_target="tpu_custom_call" | custom-call | tf_op jit(solution)/shard_map/pallas_call | solution.py:746
  82.3 0.0 copy-start
  82.4 1.3 %copy.9 = f32[16,16]{1,0:T(8,128)} copy(f32[16,16]{1,0:T(8,128)} %get-tuple-element.6) | data formatting | bytes 2048
  83.7 0.0 copy-done
  83.7 0.6 copy.10
  84.3 1.8 %copy.11 = f32[16,2,24,128]{3,2,1,0:T(8,128)} copy(f32[16,2,24,128]{3,2,1,0:T(8,128)} %get-tuple-element.8) | data formatting | bytes 786432
Async XLA Ops:
  82.3 1.3 %copy-start = (f32[16,16]{1,0:T(8,128)S(1)}, f32[16,16]{1,0:T(8,128)}, u32[]{:S(2)}) copy-start(f32[16,16]{1,0:T(8,128)} %get-tuple-element.7) | copy-start | bytes 3076

commit v3 on v2

--- a/solution.py
+++ b/solution.py
@@ -22,8 +22,8 @@
 TALL = NY + 2 * PAD
 DATA = slice(PAD, PAD + NY)
 ROWS = 8
-PIECES = ((0, 0, NY), (1, 0, ROWS), (1, ROWS, ROWS), (1, 2 * ROWS, ROWS))
 CHUNKS = NY // ROWS
+PIECES = tuple((pair, ROWS * k, ROWS) for pair in range(2) for k in range(CHUNKS))
 
 
 def steps():
@@ -58,7 +58,7 @@
 def whole_kernel(
     n_x, n_y, orb, pot, rotation_in, gram, projected, rotated,
     rotation, own_sem, ext, work, pv, edge, rt_all, fb, hb, fr, hr, h_own,
-    got, acc, acc_sent, rot, rows, back_out, back_in, part, summed, last,
+    got, acc, acc_sent, rot, rows, back_out, back_in, part, summed, last, sums, done,
     a_send, a_recv, b_send, b_recv, v_send, v_recv, d_send, d_recv,
     f_send, f_recv, h_send, h_recv, r_send, r_recv,
     right_send, right_recv, left_send, left_recv, core_send, core_recv,
@@ -563,84 +563,83 @@
             def _():
                 give_back(m, chunk).start()
 
+    def y_copy(pair, d):
+        to = lax.rem(y + d, n_y)
+        return send(
+            acc_sent.at[pair, to], part.at[pair, y],
+            y_send.at[pair, d - 1], y_recv.at[pair, d - 1], bi, to * 4 + q,
+        )
+
+    def y_begin(pair):
+        for to in range(n_y):
+            for k in range(4):
+                zh_i, x_i = (4 * to + k) // n_x, (4 * to + k) % n_x
+                acc_sent[pair, to, 4 * k : 4 * k + 4] = acc[pair, x_i, 4 * zh_i : 4 * zh_i + 4]
+        for d in sorted(range(1, n_y), key=lambda d: -min(d, n_y - d)):
+            y_copy(pair, d).start()
+        part[pair, y] = acc_sent[pair, y]
+
     acc[...] = jnp.zeros_like(acc)
     pieces = len(PIECES)
     filtered(0)
+    filtered(1)
     launch(0)
-    filtered(1)
-    later = range(1, pieces)
-
-    def serve_later(hop):
-        for piece in later:
+
+    def serve_pair(hop, pair):
+        for piece in range(CHUNKS * pair, CHUNKS * (pair + 1)):
             serve(hop, piece)
 
-    serve(1, 0)
     applied(0)
-    serve(2, 0)
+    serve_pair(1, 0)
     launch(1)
     applied(1)
-    serve(3, 0)
-    serve_later(1)
+    serve_pair(2, 0)
+    serve_pair(1, 1)
     take_applied(0)
-    serve(4, 0)
-    serve_later(2)
+    serve_pair(3, 0)
+    serve_pair(2, 1)
     take_applied(1)
     for d in range(1, ZH):
         r_wait(d)
-    take_core(0)
-    rotate(0)
-    serve_later(3)
-    correlate(0)
-    serve_later(4)
-    for piece in range(1, pieces):
+    serve_pair(4, 0)
+    serve_pair(3, 1)
+    for piece in range(CHUNKS):
+        take_core(piece)
+        rotate(piece)
+        correlate(piece)
+    serve_pair(4, 1)
+    y_begin(0)
+    for piece in range(CHUNKS, pieces):
         take_core(piece)
         if piece == pieces - 1:
             break
         rotate(piece)
-        return_rows(piece - 1)
+        return_rows(piece - CHUNKS)
         correlate(piece)
     correlate(pieces - 1)
 
-    for pair in range(2):
-        for k in range(ZH):
-            acc_sent[:, 8 * k + 4 * pair : 8 * k + 4 * pair + 4] = acc[pair, :, 4 * k : 4 * k + 4]
-
-    def columns_of(to):
-        first = 4 * to
-        return (
-            pl.ds(lax.rem(first, n_x), 4),
-            pl.ds(pl.multiple_of(first // n_x * 8, 8), 8),
-        )
-
-    def y_copy(d):
-        to = lax.rem(y + d, n_y)
-        return send(
-            acc_sent.at[columns_of(to)], part.at[y],
-            y_send.at[d - 1], y_recv.at[d - 1], bi, to * 4 + q,
-        )
-
-    for d in range(1, n_y):
-        y_copy(d).start()
-    part[y] = acc_sent[columns_of(y)]
+    y_begin(1)
     rotate(pieces - 1)
     return_rows(CHUNKS - 1)
-    for d in range(1, n_y):
-        y_copy(d).wait_recv()
-    total = part[0]
-    for k in range(1, n_y):
-        total = total + part[k]
-    summed[...] = total
-
-    def z_copy(e):
-        oz, oc, band, space = along(e)
-        return send(
-            summed.at[lax.rem(oz, 2) * 2 + oc], last.at[c, z],
-            z_send.at[e - 1], z_recv.at[e - 1], band, space,
-        )
-
-    for e in range(1, 2 * Z):
-        z_copy(e).start()
-    last[c, z] = summed[q]
+    for pair in range(2):
+        for d in range(1, n_y):
+            y_copy(pair, d).wait_recv()
+        total = part[pair, 0]
+        for k in range(1, n_y):
+            total = total + part[pair, k]
+        for k in range(4):
+            summed[k // 2, k % 2, 4 * pair : 4 * pair + 4] = total[4 * k : 4 * k + 4]
+
+    def z_copy(d):
+        oz, band, space = along_z(d)
+        return send(
+            summed.at[lax.rem(oz, 2)], last.at[z],
+            z_send.at[d - 1], z_recv.at[d - 1], band, space,
+        )
+
+    for d in far:
+        z_copy(d).start()
+    last[z] = summed[zl]
 
     for chunk in range(CHUNKS):
         for plane in range(2):
@@ -654,8 +653,20 @@
                 back_in[plane, chunk].astype(F32).reshape(16, ROWS, NZ)
             )
 
-    for e in range(1, 2 * Z):
-        z_copy(e).wait_recv()
+    for d in range(1, Z):
+        z_copy(d).wait_recv()
+    value = last[0]
+    for k in range(1, Z):
+        value = value + last[k]
+    sums[0] = value
+    done[c] = sums[0, c]
+    trade = send(
+        sums.at[0, 1 - c], done.at[c], v_send.at[4], v_recv.at[4], bi, core
+    )
+    trade.start()
+    send(
+        sums.at[0, c], done.at[1 - c], v_send.at[4], v_recv.at[4], bi, core
+    ).wait_recv()
     n = lax.broadcasted_iota(jnp.int32, (64, NZ), 0)
     l = lax.broadcasted_iota(jnp.int32, (64, NZ), 1)
     lane_of = (
@@ -664,9 +675,7 @@
     )
     picked = None
     for cls in range(2):
-        value = last[cls, 0]
-        for k in range(1, Z):
-            value = value + last[cls, k]
+        value = done[cls]
         select = jnp.where((l == lane_of) & ((n // 4) % 2 == cls), 1.0, 0.0)
         value = lax.dot_general(
             select, value, (((1,), (1,)), ((), ())),
@@ -728,10 +737,12 @@
             def _():
                 give_back(m, chunk).wait_send()
 
-    for d in range(1, n_y):
-        y_copy(d).wait_send()
-    for e in range(1, 2 * Z):
-        z_copy(e).wait_send()
+    for pair in range(2):
+        for d in range(1, n_y):
+            y_copy(pair, d).wait_send()
+    for d in range(1, Z):
+        z_copy(d).wait_send()
+    trade.wait_send()
 
 
 def shards(orbitals, potential, rotation):
@@ -766,20 +777,22 @@
             VMEM((2, NY, 2 * Z, NZ), BF16),
             VMEM((2, n_x, 2, NY, 2 * Z, NZ), BF16),
             VMEM((2, n_x, 2 * Z, NZ), F32),
-            VMEM((n_x, 4 * Z, NZ), F32),
+            VMEM((2, n_y, 16, NZ), F32),
             VMEM((NY, 32, NZ), F32),
             VMEM((ROWS, 32, NZ), F32),
             VMEM((CHUNKS, 2, 16 * ROWS, NZ), BF16),
             VMEM((2, CHUNKS, 16 * ROWS, NZ), BF16),
-            VMEM((n_y, 4, 8, NZ), F32),
-            VMEM((4, 8, NZ), F32),
-            VMEM((2, Z, 8, NZ), F32),
-            dma((2, 3)), dma((2, 3)), dma((2, 4, 2)), dma((2, 4, 2)), dma((4,)), dma((4,)),
+            VMEM((2, n_y, 16, NZ), F32),
+            VMEM((2, 2, 8, NZ), F32),
+            VMEM((Z, 2, 8, NZ), F32),
+            VMEM((1, 2, 8, NZ), F32),
+            VMEM((2, 8, NZ), F32),
+            dma((2, 3)), dma((2, 3)), dma((2, 4, 2)), dma((2, 4, 2)), dma((5,)), dma((5,)),
             dma((2, 2)), dma((2, 2)), dma((2, Z - 1)), dma((2, Z - 1)),
             dma((2, Z - 1)), dma((2, Z - 1)), dma((ZH - 1,)), dma((ZH - 1,)),
             dma((top, pieces)), dma((top, pieces)), dma((top, pieces)), dma((top, pieces)),
             dma((n_x, pieces)), dma((n_x, pieces)), dma((2, CHUNKS)), dma((2, CHUNKS)),
-            dma((n_y - 1,)), dma((n_y - 1,)), dma((2 * Z - 1,)), dma((2 * Z - 1,)),
+            dma((2, n_y - 1)), dma((2, n_y - 1)), dma((Z - 1,)), dma((Z - 1,)),
         ],
         compiler_params=pltpu.CompilerParams(
             collective_id=0, has_side_effects=True, vmem_limit_bytes=60 * 2**20

time: 86.3 us -> 82.3 us (0.954)
  Pallas kernels: 81.7 us -> 77.8 us
    pallas_call x1, Pallas kernels: 81.7 us -> 77.8 us  [shards(): pl.pallas_call(kernel, out_shape=(jax.ShapeDtypeStruct((16, 16), F32), ja...]
where the time goes in v3:
time: 82.3 us; the launch traced here: 82.1 us
  Pallas kernels  77.8 us (95%)
  local copies, waits for them, and re-layouts  3.67 us (4%)
    pallas_call x1, Pallas kernels, shards(): pl.pallas_call(kernel, out_shape=(jax.ShapeDtypeStruct((16, 16), F32), ja...  77.8 us
    unnamed x5, local copies, waits for them, and re-layouts  3.67 us

profile of v3, /device:TPU:1, one launch (start us, length us, event | category | flops | bytes accessed | tf_op | source)
XLA Modules:
  0.0 82.1 jit_solution(9292387312976527382)
XLA Ops:
  0.6 77.8 %shard_map.58 = (f32[16,16]{1,0:T(8,128)}, f32[16,16]{1,0:T(8,128)}, f32[16,2,24,128]{3,2,1,0:T(8,128)}) custom-call(f32[16,2,24,128]{3,2,1,0:T(8,128)} %refs_0_.1, f32[2,24,128]{2,1,0:T(8,128)} %refs_1_.1, f32[16,512]{1,0:T(8,128)} %bitcast.1), custom_call_target="tpu_custom_call" | custom-call | tf_op jit(solution)/shard_map/pallas_call | solution.py:757
  78.4 0.0 copy-start
  78.4 1.3 %copy.9 = f32[16,16]{1,0:T(8,128)} copy(f32[16,16]{1,0:T(8,128)} %get-tuple-element.6) | data formatting | bytes 2048
  79.7 0.0 copy-done
  79.7 0.6 copy.10
  80.3 1.8 %copy.11 = f32[16,2,24,128]{3,2,1,0:T(8,128)} copy(f32[16,2,24,128]{3,2,1,0:T(8,128)} %get-tuple-element.8) | data formatting | bytes 786432
Async XLA Ops:
  78.4 1.3 %copy-start = (f32[16,16]{1,0:T(8,128)S(1)}, f32[16,16]{1,0:T(8,128)}, u32[]{:S(2)}) copy-start(f32[16,16]{1,0:T(8,128)} %get-tuple-element.7) | copy-start | bytes 3076

commit v4 on v3

--- a/solution.py
+++ b/solution.py
@@ -757,9 +757,9 @@
     return pl.pallas_call(
         kernel,
         out_shape=(
-            jax.ShapeDtypeStruct((16, 16), F32),
-            jax.ShapeDtypeStruct((16, 16), F32),
-            jax.ShapeDtypeStruct(orbitals.shape, F32),
+            VMEM((16, 16), F32),
+            VMEM((16, 16), F32),
+            VMEM(orbitals.shape, F32),
         ),
         in_specs=[pl.BlockSpec(memory_space=pltpu.HBM)] * 3,
         out_specs=[pl.BlockSpec(memory_space=VMEM)] * 3,

time: 82.3 us -> 79.7 us (0.968)
  local copies, waits for them, and re-layouts: 3.67 us -> 1.94 us
    unnamed x5 -> x3, local copies, waits for them, and re-layouts: 3.67 us -> 1.94 us
where the time goes in v4:
time: 79.7 us; the launch traced here: 79.6 us
  Pallas kernels  77 us (97%)
  local copies, waits for them, and re-layouts  1.94 us (2%)
    pallas_call x1, Pallas kernels, shards(): pl.pallas_call(kernel, out_shape=(VMEM((16, 16), F32), VMEM((16, 16), F32...  77 us
    unnamed x3, local copies, waits for them, and re-layouts  1.94 us

profile of v4, /device:TPU:1, one launch (start us, length us, event | category | flops | bytes accessed | tf_op | source)
XLA Modules:
  0.0 79.6 jit_solution(2995563636636643387)
XLA Ops:
  0.6 77.0 %shard_map.58 = (f32[16,16]{1,0:T(8,128)S(1)}, f32[16,16]{1,0:T(8,128)S(1)}, f32[16,2,24,128]{3,2,1,0:T(8,128)S(1)}) custom-call(f32[16,2,24,128]{3,2,1,0:T(8,128)} %refs_0_.1, f32[2,24,128]{2,1,0:T(8,128)} %refs_1_.1, f32[16,512]{1,0:T(8,128)} %bitcast.1), custom_call_target="tpu_custom_call" | custom-call | tf_op jit(solution)/shard_map/pallas_call | solution.py:757
  77.6 0.6 copy.9
  78.2 0.6 copy.10
  78.8 0.7 copy.11
